TPU v7x, 128 devices: a whole 4x4x4 slice. The times are simulated.
128 devices in a mesh: wide: 16 (over z_hi, x, core), narrow: 8 (over z_lo, y).
Axes of the slice: x: 4, y: 4, z: 4 (z_hi: 2, z_lo: 2; z = z_hi * 2 + z_lo), core: 2. Of those that a mesh axis runs over, the one named last changes fastest.
Arguments:
- populations: float32 [19, 4, 1024, 2048], P(None, None, ('wide', 'narrow')), as said below
- phase: int32 [4, 1024, 2048], P(None, ('wide', 'narrow')), may hold values from 0 to 2, as said below
- porosity: float32 [4, 1024, 2048], P(None, ('wide', 'narrow')), may hold values from 0 to 1, as said below
- napl: float32 [4, 1024, 2048], P(None, ('wide', 'narrow')), may hold values from 0 to 0.9, as said below
- concentration: float32 [4, 1024, 2048], P(None, ('wide', 'narrow')), may hold values from 0 to 1
- flags: int32 [2, 4, 2048], replicated, may hold values 0 or 1
Outputs:
- populations_out: float32 [19, 4, 1024, 2048], P(None, None, ('wide', 'narrow'))
- concentration_out: float32 [4, 1024, 2048], P(None, 'wide', 'narrow')
- napl_out: float32 [4, 1024, 2048], P(None, 'wide', 'narrow')
Inputs may be any that keep to these rules, and one draw needn't show every extreme that they name: `phase`: 0 open pore, 1 pore holding NAPL, 2 solid. `porosity`: exactly 0 on voxels of phase 2 and 0.35 or more elsewhere. `napl`: above 0 exactly on voxels of phase 1, 0 elsewhere. `populations`: every entry positive.
All inputs are finite; a program needn't handle non-finite values.
Results may differ from a plain program's by a relative error of at most 0.0003.
Values sent between devices are 32-bit elements; how exact they have to be, the bound alone decides.
A program may use at most 128 MiB of HBM per device.

v0:
```python
import functools

import jax
import jax.numpy as jnp
from jax import lax
from jax.experimental import pallas as pl
from jax.experimental.pallas import tpu as pltpu
from jax.sharding import PartitionSpec as P

MESH = pl.DeviceIdType.MESH
DIRS = [
    (0, 0, 0), (1, 0, 0), (-1, 0, 0), (0, 1, 0), (0, -1, 0), (0, 0, 1), (0, 0, -1),
    (1, 1, 0), (-1, -1, 0), (1, -1, 0), (-1, 1, 0), (1, 0, 1), (-1, 0, -1), (1, 0, -1), (-1, 0, 1),
    (0, 1, 1), (0, -1, -1), (0, 1, -1), (0, -1, 1),
]
OPP = [0, 2, 1, 4, 3, 6, 5, 8, 7, 10, 9, 12, 11, 14, 13, 16, 15, 18, 17]
UP = [1, 7, 9, 11, 13]
DOWN = [2, 8, 10, 12, 14]
ORDER = UP + DOWN + [0, 3, 4, 5, 6, 15, 16, 17, 18]
SLOT = {q: i for i, q in enumerate(ORDER)}
STEPS = 4
Z = 4
R = 8
B = 128


def collide(f, phase):
    total, diff = {}, {}
    for q in range(1, 19, 2):
        total[q] = f[q] + f[q + 1]
        diff[q] = f[q] - f[q + 1]
    rho = (
        ((f[0] + total[1]) + (total[3] + total[5]))
        + ((total[7] + total[9]) + (total[11] + total[13]))
        + (total[15] + total[17])
    )
    jx = (diff[1] + diff[7]) + (diff[9] + diff[11]) + diff[13]
    jy = (diff[3] + diff[7]) + (diff[15] - diff[9]) + diff[17]
    jz = (diff[5] + diff[11]) + (diff[15] - diff[13]) - diff[17]
    rho = jnp.where(phase == 2, jnp.nan, rho)
    factor = jnp.where(phase == 1, 0.5, 1.0)
    per = factor / rho
    vx, vy, vz = jx * per, jy * per, jz * per
    factor = factor * (3.75 / 36.0)
    nx, ny, nz = jx * factor, jy * factor, jz * factor
    hx, hy, hz = vx * 1.5, vy * 1.5, vz * 1.5
    sxx, syy, szz = nx * hx, ny * hy, nz * hz
    hx, hy = hx + hx, hy + hy
    xy, xz, yz = ny * hx, nz * hx, nz * hy
    even = rho * (1.25 / 36.0) - (sxx + syy + szz) * (1.0 / 3.0)
    post = [None] * 19
    post[0] = 12.0 * even - 0.25 * f[0]

    def pair(q, e, o):
        post[q] = (e + o) - 0.25 * f[q]
        post[q + 1] = (e - o) - 0.25 * f[q + 1]

    ex, ey, ez = even + sxx, even + syy, even + szz
    pair(1, ex + ex, nx + nx)
    pair(3, ey + ey, ny + ny)
    pair(5, ez + ez, nz + nz)
    exy, exz, eyz = ex + syy, ex + szz, ey + szz
    pair(7, exy + xy, nx + ny)
    pair(9, exy - xy, nx - ny)
    pair(11, exz + xz, nx + nz)
    pair(13, exz - xz, nx - nz)
    pair(15, eyz + yz, ny + nz)
    pair(17, eyz - yz, ny - nz)
    return post


def moments(f):
    total, diff = {}, {}
    for q in range(1, 19, 2):
        total[q] = f[q] + f[q + 1]
        diff[q] = f[q] - f[q + 1]
    rho = (
        ((f[0] + total[1]) + (total[3] + total[5]))
        + ((total[7] + total[9]) + (total[11] + total[13]))
        + (total[15] + total[17])
    )
    jx = (diff[1] + diff[7]) + (diff[9] + diff[11]) + diff[13]
    jy = (diff[3] + diff[7]) + (diff[15] - diff[9]) + diff[17]
    jz = (diff[5] + diff[11]) + (diff[15] - diff[13]) - diff[17]
    return rho, jx, jy, jz


def half_minmod(p, q):
    return 0.5 * jnp.maximum(jnp.minimum(p, q), jnp.minimum(jnp.maximum(p, q), 0.0))


def face_flux(back, here, ahead, far, w, a):
    step = ahead - here
    up = here + half_minmod(here - back, step)
    down = ahead - half_minmod(step, far - ahead)
    return a * jnp.where(a > 0, up, down) - (0.15 * w) * step


def body(
    wide, narrow, width, tile,
    pop_in, phase_in, poro_in, napl_in, conc_in, flags_in,
    pop_out, conc_out, napl_out,
    fbuf, phase, poro, napl, conc, conc2, flags, post, lo, hi,
    plo, phi, clo, chi, ulo, uhi, ux, uy, uz, wx, wl, wy, wz, ax, al, ay, az, inv,
    load_sem, small_sem, out_sem, own_sem,
    send_sem, recv_sem, psend, precv, csend, crecv, usend, urecv, asend, arecv,
):
    w, n = lax.axis_index("wide"), lax.axis_index("narrow")
    chunks = narrow
    per_chunk = tile // B
    strip = w * narrow + n

    def neighbour(offset):
        g = lax.rem(strip + offset + wide * narrow, wide * narrow)
        return (g // narrow, lax.rem(g, narrow))

    after, before = neighbour(1), neighbour(-1)
    first, last = strip == 0, strip == wide * narrow - 1

    def cols(k):
        return pl.ds(pl.multiple_of(k * tile, tile), tile)

    def pcols(k):
        return pl.ds(pl.multiple_of(B + k * tile, B), tile)

    def load(k):
        return pltpu.make_async_copy(
            pop_in.at[:, :, :, cols(k)], fbuf.at[:, :, :, cols(k)], load_sem.at[k]
        )

    smalls = [
        pltpu.make_async_copy(phase_in, phase, small_sem.at[0]),
        pltpu.make_async_copy(poro_in, poro.at[:, :, pl.ds(B, width)], small_sem.at[1]),
        pltpu.make_async_copy(conc_in, conc.at[0, :, :, pl.ds(B, width)], small_sem.at[2]),
        pltpu.make_async_copy(napl_in, napl, small_sem.at[3]),
        pltpu.make_async_copy(flags_in, flags, small_sem.at[4]),
    ]
    smalls[0].start()
    load(0).start()
    for copy in smalls[1:]:
        copy.start()
    for k in range(1, chunks):
        load(k).start()

    barrier = pltpu.get_barrier_semaphore()
    pl.semaphore_signal(barrier, inc=1, device_id=after, device_id_type=MESH)
    pl.semaphore_signal(barrier, inc=1, device_id=before, device_id_type=MESH)
    for k in range(1, narrow):
        pl.semaphore_signal(
            barrier, inc=1, device_id=(w, lax.rem(n + k, narrow)), device_id_type=MESH
        )

    lane = lax.broadcasted_iota(jnp.int32, (R, B), 1)
    row = lax.broadcasted_iota(jnp.int32, (R, B), 0)
    nan = jnp.full((R, B), jnp.nan, jnp.float32)
    zero = jnp.zeros((R, B), jnp.float32)
    ends = (pl.ds(0, B), pl.ds(B + width, B))

    def fill(z, carry):
        for end in ends:
            for p in range(2):
                for q in range(19):
                    if DIRS[q][1]:
                        post[p, SLOT[q], z, :, end] = nan
            for s in range(STEPS):
                for m in (1, 2):
                    lo[s, m, z, :, end] = nan
                    hi[s, m, z, :, end] = nan
            poro[z, :, end] = zero
            uy[z, :, end] = zero
            for p in range(2):
                conc[p, z, :, end] = zero
        return carry

    lax.fori_loop(0, Z, fill, 0)

    def edge(s, side, k):
        p = lax.rem(s, 2)
        if side == 0:
            src = post.at[p, pl.ds(0, 5), :, pl.ds(R - 1, 1), pcols(k)]
            dst = lo.at[s, :, :, pl.ds(R - 1, 1), pcols(k)]
        else:
            src = post.at[p, pl.ds(5, 5), :, pl.ds(0, 1), pcols(k)]
            dst = hi.at[s, :, :, pl.ds(0, 1), pcols(k)]
        return pltpu.make_async_remote_copy(
            src_ref=src, dst_ref=dst, send_sem=send_sem.at[s, side, k], recv_sem=recv_sem.at[s, side, k],
            device_id=after if side == 0 else before, device_id_type=MESH,
        )

    def poro_edge(side):
        rows = pl.ds(R - 1, 1) if side == 0 else pl.ds(0, 1)
        inner = pl.ds(B, width)
        return pltpu.make_async_remote_copy(
            src_ref=poro.at[:, rows, inner], dst_ref=(plo if side == 0 else phi).at[:, rows, :],
            send_sem=psend.at[side], recv_sem=precv.at[side],
            device_id=after if side == 0 else before, device_id_type=MESH,
        )

    def conc_edge(p, side, k):
        rows = pl.ds(R - 2, 2) if side == 0 else pl.ds(0, 2)
        return pltpu.make_async_remote_copy(
            src_ref=conc.at[p, :, rows, pcols(k)], dst_ref=(clo if side == 0 else chi).at[p, :, rows, cols(k)],
            send_sem=csend.at[p, side, k], recv_sem=crecv.at[p, side, k],
            device_id=after if side == 0 else before, device_id_type=MESH,
        )

    def vel_edge(side, k):
        rows = pl.ds(R - 1, 1) if side == 0 else pl.ds(0, 1)
        return pltpu.make_async_remote_copy(
            src_ref=ux.at[:, rows, cols(k)], dst_ref=(ulo if side == 0 else uhi).at[:, rows, cols(k)],
            send_sem=usend.at[side, k], recv_sem=urecv.at[side, k],
            device_id=after if side == 0 else before, device_id_type=MESH,
        )

    def to_tile(a, k):
        src, dst = (napl, napl_out) if a == 0 else (conc2, conc_out)
        rows = pl.ds(pl.multiple_of(n * R, R), R)
        return pltpu.make_async_remote_copy(
            src_ref=src.at[:, :, cols(k)], dst_ref=dst.at[:, rows, :],
            send_sem=asend.at[a, k], recv_sem=arecv.at[a, n], device_id=(w, k), device_id_type=MESH,
        )

    def from_tile(a, k):
        src, dst = (napl, napl_out) if a == 0 else (conc2, conc_out)
        rows = pl.ds(pl.multiple_of(k * R, R), R)
        return pltpu.make_async_remote_copy(
            src_ref=src.at[:, :, cols(k)], dst_ref=dst.at[:, rows, :],
            send_sem=asend.at[a, k], recv_sem=arecv.at[a, k], device_id=(w, k), device_id_type=MESH,
        )

    def own_tile(a):
        src, dst = (napl, napl_out) if a == 0 else (conc2, conc_out)
        rows = pl.ds(pl.multiple_of(n * R, R), R)
        return pltpu.make_async_copy(src.at[:, :, cols(n)], dst.at[:, rows, :], own_sem.at[a])

    def send_tile(a, k):
        @pl.when(k != n)
        def _():
            to_tile(a, k).start()

        @pl.when(k == n)
        def _():
            own_tile(a).start()

    def blocks(k, fn, carry=0):
        return lax.fori_loop(0, per_chunk, lambda i, c: fn(k * per_chunk + i, c), carry)

    def at(b):
        return pl.ds(pl.multiple_of(b * B, B), B)

    def start_block(b, carry):
        here, there = at(b), at(b + 1)
        for z in range(Z):
            f = [fbuf[q, z, :, here] for q in range(19)]
            out = collide(f, phase[z, :, here])
            for q in range(19):
                post[0, SLOT[q], z, :, there] = out[q]
        return carry

    smalls[0].wait()
    load(0).wait()
    blocks(0, start_block)
    pl.semaphore_wait(barrier, narrow + 1)
    for side in range(2):
        edge(0, side, 0).start()
    for copy in smalls[1:3]:
        copy.wait()
    for side in range(2):
        poro_edge(side).start()

    def first_chunk(k, carry):
        load(k).wait()
        blocks(k, start_block)
        for side in range(2):
            edge(0, side, k).start()
        return carry

    lax.fori_loop(1, chunks, first_chunk, 0)
    for side in range(2):
        for k in range(chunks):
            conc_edge(0, side, k).start()
    for copy in smalls[3:]:
        copy.wait()

    def stream(p, s, z, b):
        base = b * B + B

        def block(slot, layer, shift, ex):
            where = pl.ds(pl.multiple_of(base + shift, B), B)
            value = post[p, slot, layer, :, where]
            if ex == 1:
                value = jnp.where(row == R - 1, lo[s, slot, layer, :, where], value)
            elif ex == -1:
                value = jnp.where(row == 0, hi[s, slot - 5, layer, :, where], value)
            return value

        here = pl.ds(pl.multiple_of(base, B), B)
        f = []
        for q in range(19):
            ex, ey, ez = DIRS[q]
            slot, layer = SLOT[q], (z - ez) % Z
            if q == 0:
                f.append(post[p, slot, z, :, here])
                continue
            moved = block(slot, layer, 0, ex)
            if ey == 1:
                moved = pltpu.roll(jnp.where(lane == B - 1, block(slot, layer, -B, ex), moved), 1, 1)
            elif ey == -1:
                moved = pltpu.roll(jnp.where(lane == 0, block(slot, layer, B, ex), moved), B - 1, 1)
            if ex:
                moved = pltpu.roll(moved, 1 if ex == 1 else R - 1, 0)
            f.append(jnp.where(moved < jnp.inf, moved, post[p, SLOT[OPP[q]], z, :, here]))
        return f

    def await_edges(s, k):
        @pl.when(k == 0)
        def _():
            for side in range(2):
                edge(s, side, k).wait_recv()

        @pl.when(k < chunks - 1)
        def _():
            for side in range(2):
                edge(s, side, k + 1).wait_recv()

    def one_step(s, carry):
        old, new = lax.rem(s + 1, 2), lax.rem(s, 2)

        def move_block(b, c):
            for z in range(Z):
                out = collide(stream(old, s - 1, z, b), phase[z, :, at(b)])
                for q in range(19):
                    post[new, SLOT[q], z, :, at(b + 1)] = out[q]
            return c

        def chunk(k, c):
            await_edges(s - 1, k)

            @pl.when(s >= 2)
            def _():
                for side in range(2):
                    edge(s - 2, side, k).wait_send()

            blocks(k, move_block)
            for side in range(2):
                edge(s, side, k).start()
            return c

        lax.fori_loop(0, chunks, chunk, 0)

        @pl.when(s == 1)
        def _():
            for side in range(2):
                poro_edge(side).wait_recv()

            def coef(b, c):
                here, there, beyond = at(b), at(b + 1), at(b + 2)
                for z in range(Z):
                    own = poro[z, :, there]
                    high = jnp.where(last, flags[1, z : z + 1, here].astype(jnp.float32), phi[z, :, here])
                    low = jnp.where(first, flags[0, z : z + 1, here].astype(jnp.float32), plo[z, :, here])
                    wx[z, :, here] = own * pltpu.roll(jnp.where(row == 0, high, own), R - 1, 0)
                    wl[z, :, here] = low * pltpu.roll(own, R - 1, 0)
                    wy[z, :, here] = own * pltpu.roll(jnp.where(lane == 0, poro[z, :, beyond], own), B - 1, 1)
                    wz[z, :, here] = own * poro[(z + 1) % Z, :, there]
                    inv[z, :, here] = 1.0 / jnp.maximum(own, 0.3)
                return c

            lax.fori_loop(0, width // B, coef, 0)

        return carry

    lax.fori_loop(1, STEPS, one_step, 0)

    def last_block(b, carry):
        here, there = at(b), at(b + 1)
        for z in range(Z):
            f = stream((STEPS - 1) % 2, STEPS - 1, z, b)
            solid = phase[z, :, here] == 2
            rho, jx, jy, jz = moments(f)
            per = jnp.where(solid, 0.0, 1.0) / jnp.where(solid, 1.0, rho)
            ux[z, :, here] = jnp.where(solid, 0.0, jx * per)
            uy[z, :, there] = jnp.where(solid, 0.0, jy * per)
            uz[z, :, here] = jnp.where(solid, 0.0, jz * per)
            for q in range(19):
                fbuf[q, z, :, here] = jnp.where(solid, fbuf[q, z, :, here], f[q])
        return carry

    def store(k):
        return pltpu.make_async_copy(
            fbuf.at[:, :, :, cols(k)], pop_out.at[:, :, :, cols(k)], out_sem.at[k]
        )

    def last_chunk(k, carry):
        await_edges(STEPS - 1, k)
        blocks(k, last_block)
        for side in range(2):
            vel_edge(side, k).start()
        store(k).start()
        return carry

    lax.fori_loop(0, chunks, last_chunk, 0)

    def transport(step, b, carry):
        here, there, back, beyond = at(b), at(b + 1), at(b), at(b + 2)
        c = [conc[step, z, :, there] for z in range(Z)]
        if step == 0:
            for z in range(Z):
                vx = ux[z, :, here]
                high = jnp.where(last, pltpu.roll(vx, 1, 0), uhi[z, :, here])
                low = jnp.where(first, pltpu.roll(vx, R - 1, 0), ulo[z, :, here])
                nxt = pltpu.roll(vx, R - 1, 0)
                ax[z, :, here] = wx[z, :, here] * (0.5 * (vx + jnp.where(row == R - 1, pltpu.roll(high, R - 1, 0), nxt)))
                al[z, :, here] = wl[z, :, here] * (0.5 * (low + nxt))
                vy = uy[z, :, there]
                ay[z, :, here] = wy[z, :, here] * (
                    0.5 * (vy + pltpu.roll(jnp.where(lane == 0, uy[z, :, beyond], vy), B - 1, 1))
                )
                az[z, :, here] = wz[z, :, here] * (0.5 * (uz[z, :, here] + uz[(z + 1) % Z, :, here]))
        zflux = [
            face_flux(
                c[(z - 1) % Z], c[z], c[(z + 1) % Z], c[(z + 2) % Z], wz[z, :, here], az[z, :, here]
            )
            for z in range(Z)
        ]
        flow = []
        for z in range(Z):
            own = c[z]
            high = chi[step, z, :, here]
            low = clo[step, z, :, here]
            up1, up2 = pltpu.roll(own, R - 1, 0), pltpu.roll(own, R - 2, 0)
            low = jnp.where(first, 0.0, low)
            down1 = pltpu.roll(jnp.where(row == R - 1, low, own), 1, 0)
            end = pltpu.roll(own, 1, 0)
            one = jnp.where(last, end, high)
            two = jnp.where(last, jnp.where(row == 0, end, pltpu.roll(own, 2, 0)), high)
            ahead = pltpu.roll(jnp.where(row == 0, one, own), R - 1, 0)
            far = pltpu.roll(jnp.where(row < 2, two, own), R - 2, 0)
            xflux = face_flux(down1, own, ahead, far, wx[z, :, here], ax[z, :, here])
            xlow = face_flux(pltpu.roll(low, 1, 0), low, up1, up2, wl[z, :, here], al[z, :, here])
            change = pltpu.roll(jnp.where(row == R - 1, xlow, xflux), 1, 0) - xflux
            cb, cn = conc[step, z, :, back], conc[step, z, :, beyond]
            left = pltpu.roll(jnp.where(lane == B - 1, cb, own), 1, 1)
            right = pltpu.roll(jnp.where(lane == 0, cn, own), B - 1, 1)
            right2 = pltpu.roll(jnp.where(lane < 2, cn, own), B - 2, 1)
            yflux = face_flux(left, own, right, right2, wy[z, :, here], ay[z, :, here])
            flow.append(yflux)
            change = change + (pltpu.roll(jnp.where(lane == B - 1, carry[z], yflux), 1, 1) - yflux)
            change = change + (zflux[(z - 1) % Z] - zflux[z])
            s = napl[z, :, here]
            if step == 0:
                rate = 0.3 * s * (1.0 - own)
                new = own + (change + rate) * inv[z, :, here]
                conc[1, z, :, there] = new
                s = s - 0.5 * rate
                rate = 0.3 * s * (1.0 - new)
                napl[z, :, here] = s - 0.5 * rate
                conc2[z, :, here] = rate
            else:
                conc2[z, :, here] = own + (change + conc2[z, :, here]) * inv[z, :, here]
        return tuple(flow)

    def first_transport(k, carry):
        for side in range(2):
            vel_edge(side, k).wait_recv()
            conc_edge(0, side, k).wait_recv()
        carry = blocks(k, functools.partial(transport, 0), carry)
        for side in range(2):
            conc_edge(1, side, k).start()
        send_tile(0, k)
        return carry

    def second_transport(k, carry):
        for side in range(2):
            conc_edge(1, side, k).wait_recv()
        carry = blocks(k, functools.partial(transport, 1), carry)
        send_tile(1, k)
        return carry

    still = (zero,) * Z
    lax.fori_loop(0, chunks, first_transport, still)
    lax.fori_loop(0, chunks, second_transport, still)

    def settle(k, carry):
        for side in range(2):
            for s in (STEPS - 2, STEPS - 1):
                edge(s, side, k).wait_send()
            vel_edge(side, k).wait_send()
            for p in range(2):
                conc_edge(p, side, k).wait_send()
        store(k).wait()
        return carry

    lax.fori_loop(0, chunks, settle, 0)
    for side in range(2):
        poro_edge(side).wait_send()

    def settle_tile(k, carry):
        @pl.when(k != n)
        def _():
            for a in range(2):
                to_tile(a, k).wait_send()
                from_tile(a, k).wait_recv()

        return carry

    lax.fori_loop(0, chunks, settle_tile, 0)
    for a in range(2):
        own_tile(a).wait()


def local(wide, narrow, populations, phase, porosity, napl, concentration, flags):
    width = phase.shape[2]
    tile = width // narrow
    padded = width + 2 * B
    f32 = jnp.float32
    DMA = pltpu.SemaphoreType.DMA

    def full():
        return pltpu.VMEM((Z, R, width), f32)

    any_space = pl.BlockSpec(memory_space=pl.ANY)
    scratch = [
        pltpu.VMEM((19, Z, R, width), f32),
        pltpu.VMEM((Z, R, width), jnp.int32),
        pltpu.VMEM((Z, R, padded), f32),
        full(),
        pltpu.VMEM((2, Z, R, padded), f32),
        full(),
        pltpu.VMEM((2, Z, width), jnp.int32),
        pltpu.VMEM((2, 19, Z, R, padded), f32),
        pltpu.VMEM((STEPS, 5, Z, R, padded), f32),
        pltpu.VMEM((STEPS, 5, Z, R, padded), f32),
        full(), full(),
        pltpu.VMEM((2, Z, R, width), f32), pltpu.VMEM((2, Z, R, width), f32),
        full(), full(),
        full(), pltpu.VMEM((Z, R, padded), f32), full(),
        full(), full(), full(), full(),
        full(), full(), full(), full(),
        full(),
        DMA((narrow,)), DMA((5,)), DMA((narrow,)), DMA((2,)),
        DMA((STEPS, 2, narrow)), DMA((STEPS, 2, narrow)),
        DMA((2,)), DMA((2,)),
        DMA((2, 2, narrow)), DMA((2, 2, narrow)),
        DMA((2, narrow)), DMA((2, narrow)),
        DMA((2, narrow)), DMA((2, narrow)),
    ]
    tiles = jax.ShapeDtypeStruct((Z, R * narrow, tile), f32)
    return pl.pallas_call(
        functools.partial(body, wide, narrow, width, tile),
        out_shape=(jax.ShapeDtypeStruct(populations.shape, f32), tiles, tiles),
        in_specs=[any_space] * 6,
        out_specs=(any_space,) * 3,
        scratch_shapes=scratch,
        compiler_params=pltpu.CompilerParams(
            collective_id=0, has_side_effects=True, vmem_limit_bytes=56 * 2**20
        ),
        name="dissolution",
    )(populations, phase, porosity, napl, concentration, flags)


def solution(mesh):
    strips = ("wide", "narrow")
    in_specs = (
        P(None, None, strips, None),
        P(None, strips, None),
        P(None, strips, None),
        P(None, strips, None),
        P(None, strips, None),
        P(),
    )
    out_specs = (
        P(None, None, strips, None),
        P(None, "wide", "narrow"),
        P(None, "wide", "narrow"),
    )
    fn = functools.partial(local, mesh.shape["wide"], mesh.shape["narrow"])
    return jax.shard_map(fn, mesh=mesh, in_specs=in_specs, out_specs=out_specs, check_vma=False)
```

profile of v0, /device:TPU:56, one launch (start us, length us, event | category | flops | bytes accessed | tf_op | source)
XLA Modules:
  0.0 69.6 jit_solution(622347723718146334)
XLA Ops:
  0.6 62.2 %dissolution.1 = (f32[19,4,8,2048]{3,2,1,0:T(8,128)}, f32[4,64,256]{2,1,0:T(8,128)}, f32[4,64,256]{2,1,0:T(8,128)}) custom-call(f32[19,4,8,2048]{3,2,1,0:T(8,128)} %pop_in.1, s32[4,8,2048]{2,1,0:T(8,128)} %phase_in.1, f32[4,8,2048]{2,1,0:T(8,128)} %poro_in.1, f32[4,8,2048]{2,1,0:T(8,128)} %napl_in.1, f32[4,8,2048]{2,1,0:T(8,128)} %conc_in.1, ...), custom_call_target="tpu_custom_call" | custom-call | tf_op jit(solution)/shard_map/dissolution/pallas_call | solution.py:549
  62.8 0.0 copy-start.1
  62.8 0.0 copy-start
  62.8 5.3 %copy.12 = f32[19,4,8,2048]{3,2,1,0:T(8,128)} copy(f32[19,4,8,2048]{3,2,1,0:T(8,128)} %get-tuple-element.6) | data formatting | bytes 9961472
  68.2 0.0 copy-done.1
  68.2 0.7 %copy.13 = f32[4,64,256]{2,1,0:T(8,128)} copy(f32[4,64,256]{2,1,0:T(8,128)S(1)} %copy-done.1) | data formatting | bytes 524288
  68.9 0.0 copy-done
  68.9 0.7 %copy.14 = f32[4,64,256]{2,1,0:T(8,128)} copy(f32[4,64,256]{2,1,0:T(8,128)S(1)} %copy-done) | data formatting | bytes 524288
Async XLA Ops:
  62.8 5.4 %copy-start.1 = (f32[4,64,256]{2,1,0:T(8,128)S(1)}, f32[4,64,256]{2,1,0:T(8,128)}, u32[]{:S(2)}) copy-start(f32[4,64,256]{2,1,0:T(8,128)} %get-tuple-element.7) | copy-start | bytes 786436
  62.8 6.1 %copy-start = (f32[4,64,256]{2,1,0:T(8,128)S(1)}, f32[4,64,256]{2,1,0:T(8,128)}, u32[]{:S(2)}) copy-start(f32[4,64,256]{2,1,0:T(8,128)} %get-tuple-element.8) | copy-start | bytes 786436
where the time goes:
time: 69.7 us; the launch traced here: 69.6 us
  Pallas kernels  62.2 us (89%)
  local copies, waits for them, and re-layouts  6.76 us (10%)
    pallas_call x1, Pallas kernels, local(): pl.pallas_call(functools.partial(body, wide, narrow, width, tile), out_sh...  62.2 us
    unnamed x7, local copies, waits for them, and re-layouts  6.76 us

commit v1 on v0

--- a/solution.py
+++ b/solution.py
@@ -100,11 +100,12 @@
     wide, narrow, width, tile,
     pop_in, phase_in, poro_in, napl_in, conc_in, flags_in,
     pop_out, conc_out, napl_out,
-    fbuf, phase, poro, napl, conc, conc2, flags, post, lo, hi,
+    fbuf, phase, poro, napl, conc0, conc1, conc2, rate_buf, flags, post0, post1, lo, hi,
     plo, phi, clo, chi, ulo, uhi, ux, uy, uz, wx, wl, wy, wz, ax, al, ay, az, inv,
     load_sem, small_sem, out_sem, own_sem,
     send_sem, recv_sem, psend, precv, csend, crecv, usend, urecv, asend, arecv,
 ):
+    posts, concs = (post0, post1), (conc0, conc1)
     w, n = lax.axis_index("wide"), lax.axis_index("narrow")
     chunks = narrow
     per_chunk = tile // B
@@ -131,7 +132,7 @@
     smalls = [
         pltpu.make_async_copy(phase_in, phase, small_sem.at[0]),
         pltpu.make_async_copy(poro_in, poro.at[:, :, pl.ds(B, width)], small_sem.at[1]),
-        pltpu.make_async_copy(conc_in, conc.at[0, :, :, pl.ds(B, width)], small_sem.at[2]),
+        pltpu.make_async_copy(conc_in, conc0.at[:, :, pl.ds(B, width)], small_sem.at[2]),
         pltpu.make_async_copy(napl_in, napl, small_sem.at[3]),
         pltpu.make_async_copy(flags_in, flags, small_sem.at[4]),
     ]
@@ -161,7 +162,7 @@
             for p in range(2):
                 for q in range(19):
                     if DIRS[q][1]:
-                        post[p, SLOT[q], z, :, end] = nan
+                        posts[p][SLOT[q], z, :, end] = nan
             for s in range(STEPS):
                 for m in (1, 2):
                     lo[s, m, z, :, end] = nan
@@ -169,18 +170,18 @@
             poro[z, :, end] = zero
             uy[z, :, end] = zero
             for p in range(2):
-                conc[p, z, :, end] = zero
+                concs[p][z, :, end] = zero
         return carry
 
     lax.fori_loop(0, Z, fill, 0)
 
     def edge(s, side, k):
-        p = lax.rem(s, 2)
+        post = posts[s % 2]
         if side == 0:
-            src = post.at[p, pl.ds(0, 5), :, pl.ds(R - 1, 1), pcols(k)]
+            src = post.at[pl.ds(0, 5), :, pl.ds(R - 1, 1), pcols(k)]
             dst = lo.at[s, :, :, pl.ds(R - 1, 1), pcols(k)]
         else:
-            src = post.at[p, pl.ds(5, 5), :, pl.ds(0, 1), pcols(k)]
+            src = post.at[pl.ds(5, 5), :, pl.ds(0, 1), pcols(k)]
             dst = hi.at[s, :, :, pl.ds(0, 1), pcols(k)]
         return pltpu.make_async_remote_copy(
             src_ref=src, dst_ref=dst, send_sem=send_sem.at[s, side, k], recv_sem=recv_sem.at[s, side, k],
@@ -199,7 +200,7 @@
     def conc_edge(p, side, k):
         rows = pl.ds(R - 2, 2) if side == 0 else pl.ds(0, 2)
         return pltpu.make_async_remote_copy(
-            src_ref=conc.at[p, :, rows, pcols(k)], dst_ref=(clo if side == 0 else chi).at[p, :, rows, cols(k)],
+            src_ref=concs[p].at[:, rows, pcols(k)], dst_ref=(clo if side == 0 else chi).at[p, :, rows, cols(k)],
             send_sem=csend.at[p, side, k], recv_sem=crecv.at[p, side, k],
             device_id=after if side == 0 else before, device_id_type=MESH,
         )
@@ -254,7 +255,7 @@
             f = [fbuf[q, z, :, here] for q in range(19)]
             out = collide(f, phase[z, :, here])
             for q in range(19):
-                post[0, SLOT[q], z, :, there] = out[q]
+                post0[SLOT[q], z, :, there] = out[q]
         return carry
 
     smalls[0].wait()
@@ -282,12 +283,12 @@
     for copy in smalls[3:]:
         copy.wait()
 
-    def stream(p, s, z, b):
+    def stream(post, s, z, b):
         base = b * B + B
 
         def block(slot, layer, shift, ex):
             where = pl.ds(pl.multiple_of(base + shift, B), B)
-            value = post[p, slot, layer, :, where]
+            value = post[slot, layer, :, where]
             if ex == 1:
                 value = jnp.where(row == R - 1, lo[s, slot, layer, :, where], value)
             elif ex == -1:
@@ -300,7 +301,7 @@
             ex, ey, ez = DIRS[q]
             slot, layer = SLOT[q], (z - ez) % Z
             if q == 0:
-                f.append(post[p, slot, z, :, here])
+                f.append(post[slot, z, :, here])
                 continue
             moved = block(slot, layer, 0, ex)
             if ey == 1:
@@ -309,7 +310,7 @@
                 moved = pltpu.roll(jnp.where(lane == 0, block(slot, layer, B, ex), moved), B - 1, 1)
             if ex:
                 moved = pltpu.roll(moved, 1 if ex == 1 else R - 1, 0)
-            f.append(jnp.where(moved < jnp.inf, moved, post[p, SLOT[OPP[q]], z, :, here]))
+            f.append(jnp.where(moved < jnp.inf, moved, post[SLOT[OPP[q]], z, :, here]))
         return f
 
     def await_edges(s, k):
@@ -323,21 +324,20 @@
             for side in range(2):
                 edge(s, side, k + 1).wait_recv()
 
-    def one_step(s, carry):
-        old, new = lax.rem(s + 1, 2), lax.rem(s, 2)
+    def one_step(s):
+        old, new = posts[(s + 1) % 2], posts[s % 2]
 
         def move_block(b, c):
             for z in range(Z):
                 out = collide(stream(old, s - 1, z, b), phase[z, :, at(b)])
                 for q in range(19):
-                    post[new, SLOT[q], z, :, at(b + 1)] = out[q]
+                    new[SLOT[q], z, :, at(b + 1)] = out[q]
             return c
 
         def chunk(k, c):
             await_edges(s - 1, k)
 
-            @pl.when(s >= 2)
-            def _():
+            if s >= 2:
                 for side in range(2):
                     edge(s - 2, side, k).wait_send()
 
@@ -348,8 +348,7 @@
 
         lax.fori_loop(0, chunks, chunk, 0)
 
-        @pl.when(s == 1)
-        def _():
+        if s == 1:
             for side in range(2):
                 poro_edge(side).wait_recv()
 
@@ -368,14 +367,13 @@
 
             lax.fori_loop(0, width // B, coef, 0)
 
-        return carry
-
-    lax.fori_loop(1, STEPS, one_step, 0)
+    for s in range(1, STEPS):
+        one_step(s)
 
     def last_block(b, carry):
         here, there = at(b), at(b + 1)
         for z in range(Z):
-            f = stream((STEPS - 1) % 2, STEPS - 1, z, b)
+            f = stream(posts[(STEPS - 1) % 2], STEPS - 1, z, b)
             solid = phase[z, :, here] == 2
             rho, jx, jy, jz = moments(f)
             per = jnp.where(solid, 0.0, 1.0) / jnp.where(solid, 1.0, rho)
@@ -403,7 +401,8 @@
 
     def transport(step, b, carry):
         here, there, back, beyond = at(b), at(b + 1), at(b), at(b + 2)
-        c = [conc[step, z, :, there] for z in range(Z)]
+        conc = concs[step]
+        c = [conc[z, :, there] for z in range(Z)]
         if step == 0:
             for z in range(Z):
                 vx = ux[z, :, here]
@@ -439,7 +438,7 @@
             xflux = face_flux(down1, own, ahead, far, wx[z, :, here], ax[z, :, here])
             xlow = face_flux(pltpu.roll(low, 1, 0), low, up1, up2, wl[z, :, here], al[z, :, here])
             change = pltpu.roll(jnp.where(row == R - 1, xlow, xflux), 1, 0) - xflux
-            cb, cn = conc[step, z, :, back], conc[step, z, :, beyond]
+            cb, cn = conc[z, :, back], conc[z, :, beyond]
             left = pltpu.roll(jnp.where(lane == B - 1, cb, own), 1, 1)
             right = pltpu.roll(jnp.where(lane == 0, cn, own), B - 1, 1)
             right2 = pltpu.roll(jnp.where(lane < 2, cn, own), B - 2, 1)
@@ -451,13 +450,13 @@
             if step == 0:
                 rate = 0.3 * s * (1.0 - own)
                 new = own + (change + rate) * inv[z, :, here]
-                conc[1, z, :, there] = new
+                conc1[z, :, there] = new
                 s = s - 0.5 * rate
                 rate = 0.3 * s * (1.0 - new)
                 napl[z, :, here] = s - 0.5 * rate
-                conc2[z, :, here] = rate
+                rate_buf[z, :, here] = rate
             else:
-                conc2[z, :, here] = own + (change + conc2[z, :, here]) * inv[z, :, here]
+                conc2[z, :, here] = own + (change + rate_buf[z, :, here]) * inv[z, :, here]
         return tuple(flow)
 
     def first_transport(k, carry):
@@ -525,10 +524,10 @@
         pltpu.VMEM((Z, R, width), jnp.int32),
         pltpu.VMEM((Z, R, padded), f32),
         full(),
-        pltpu.VMEM((2, Z, R, padded), f32),
-        full(),
+        pltpu.VMEM((Z, R, padded), f32), pltpu.VMEM((Z, R, padded), f32),
+        full(), full(),
         pltpu.VMEM((2, Z, width), jnp.int32),
-        pltpu.VMEM((2, 19, Z, R, padded), f32),
+        pltpu.VMEM((19, Z, R, padded), f32), pltpu.VMEM((19, Z, R, padded), f32),
         pltpu.VMEM((STEPS, 5, Z, R, padded), f32),
         pltpu.VMEM((STEPS, 5, Z, R, padded), f32),
         full(), full(),

time: 69.7 us -> 57.1 us (0.82)
  Pallas kernels: 62.2 us -> 49.6 us
    pallas_call x1, Pallas kernels: 62.2 us -> 49.6 us  [local(): pl.pallas_call(functools.partial(body, wide, narrow, width, tile), out_sh...]
where the time goes in v1:
time: 57.1 us; the launch traced here: 57 us
  Pallas kernels  49.6 us (87%)
  local copies, waits for them, and re-layouts  6.76 us (12%)
  between operations  0.66 us (1%)
    pallas_call x1, Pallas kernels, local(): pl.pallas_call(functools.partial(body, wide, narrow, width, tile), out_sh...  49.6 us
    unnamed x7, local copies, waits for them, and re-layouts  6.76 us

profile of v1, /device:TPU:56, one launch (start us, length us, event | category | flops | bytes accessed | tf_op | source)
XLA Modules:
  0.0 57.0 jit_solution(10060304615355373908)
XLA Ops:
  0.6 49.6 %dissolution.1 = (f32[19,4,8,2048]{3,2,1,0:T(8,128)}, f32[4,64,256]{2,1,0:T(8,128)}, f32[4,64,256]{2,1,0:T(8,128)}) custom-call(f32[19,4,8,2048]{3,2,1,0:T(8,128)} %pop_in.1, s32[4,8,2048]{2,1,0:T(8,128)} %phase_in.1, f32[4,8,2048]{2,1,0:T(8,128)} %poro_in.1, f32[4,8,2048]{2,1,0:T(8,128)} %napl_in.1, f32[4,8,2048]{2,1,0:T(8,128)} %conc_in.1, ...), custom_call_target="tpu_custom_call" | custom-call | tf_op jit(solution)/shard_map/dissolution/pallas_call | solution.py:548
  50.2 0.0 copy-start.1
  50.2 0.0 copy-start
  50.2 5.3 %copy.12 = f32[19,4,8,2048]{3,2,1,0:T(8,128)} copy(f32[19,4,8,2048]{3,2,1,0:T(8,128)} %get-tuple-element.6) | data formatting | bytes 9961472
  55.6 0.0 copy-done.1
  55.6 0.7 %copy.13 = f32[4,64,256]{2,1,0:T(8,128)} copy(f32[4,64,256]{2,1,0:T(8,128)S(1)} %copy-done.1) | data formatting | bytes 524288
  56.3 0.0 copy-done
  56.3 0.7 %copy.14 = f32[4,64,256]{2,1,0:T(8,128)} copy(f32[4,64,256]{2,1,0:T(8,128)S(1)} %copy-done) | data formatting | bytes 524288
Async XLA Ops:
  50.2 5.4 %copy-start.1 = (f32[4,64,256]{2,1,0:T(8,128)S(1)}, f32[4,64,256]{2,1,0:T(8,128)}, u32[]{:S(2)}) copy-start(f32[4,64,256]{2,1,0:T(8,128)} %get-tuple-element.7) | copy-start | bytes 786436
  50.2 6.1 %copy-start = (f32[4,64,256]{2,1,0:T(8,128)S(1)}, f32[4,64,256]{2,1,0:T(8,128)}, u32[]{:S(2)}) copy-start(f32[4,64,256]{2,1,0:T(8,128)} %get-tuple-element.8) | copy-start | bytes 786436

commit v2 on v1

--- a/solution.py
+++ b/solution.py
@@ -19,6 +19,7 @@
 ORDER = UP + DOWN + [0, 3, 4, 5, 6, 15, 16, 17, 18]
 SLOT = {q: i for i, q in enumerate(ORDER)}
 STEPS = 4
+PARTS = 8
 Z = 4
 R = 8
 B = 128
@@ -100,15 +101,17 @@
     wide, narrow, width, tile,
     pop_in, phase_in, poro_in, napl_in, conc_in, flags_in,
     pop_out, conc_out, napl_out,
-    fbuf, phase, poro, napl, conc0, conc1, conc2, rate_buf, flags, post0, post1, lo, hi,
+    fbuf, phase, poro, napl, conc0, conc1, conc2, napl2, rate_buf, inner, flags, post0, post1, lo, hi,
     plo, phi, clo, chi, ulo, uhi, ux, uy, uz, wx, wl, wy, wz, ax, al, ay, az, inv,
-    load_sem, small_sem, out_sem, own_sem,
+    load_sem, small_sem, own_sem,
     send_sem, recv_sem, psend, precv, csend, crecv, usend, urecv, asend, arecv,
 ):
     posts, concs = (post0, post1), (conc0, conc1)
     w, n = lax.axis_index("wide"), lax.axis_index("narrow")
     chunks = narrow
     per_chunk = tile // B
+    parts = PARTS
+    part = width // parts
     strip = w * narrow + n
 
     def neighbour(offset):
@@ -117,6 +120,9 @@
 
     after, before = neighbour(1), neighbour(-1)
     first, last = strip == 0, strip == wide * narrow - 1
+
+    def part_cols(k):
+        return pl.ds(pl.multiple_of(B + k * part, B), part)
 
     def cols(k):
         return pl.ds(pl.multiple_of(k * tile, tile), tile)
@@ -178,11 +184,11 @@
     def edge(s, side, k):
         post = posts[s % 2]
         if side == 0:
-            src = post.at[pl.ds(0, 5), :, pl.ds(R - 1, 1), pcols(k)]
-            dst = lo.at[s, :, :, pl.ds(R - 1, 1), pcols(k)]
+            src = post.at[pl.ds(0, 5), :, pl.ds(R - 1, 1), part_cols(k)]
+            dst = lo.at[s, :, :, pl.ds(R - 1, 1), part_cols(k)]
         else:
-            src = post.at[pl.ds(5, 5), :, pl.ds(0, 1), pcols(k)]
-            dst = hi.at[s, :, :, pl.ds(0, 1), pcols(k)]
+            src = post.at[pl.ds(5, 5), :, pl.ds(0, 1), part_cols(k)]
+            dst = hi.at[s, :, :, pl.ds(0, 1), part_cols(k)]
         return pltpu.make_async_remote_copy(
             src_ref=src, dst_ref=dst, send_sem=send_sem.at[s, side, k], recv_sem=recv_sem.at[s, side, k],
             device_id=after if side == 0 else before, device_id_type=MESH,
@@ -199,8 +205,9 @@
 
     def conc_edge(p, side, k):
         rows = pl.ds(R - 2, 2) if side == 0 else pl.ds(0, 2)
+        src, dst = (pl.ds(B, width), pl.ds(0, width)) if p == 0 else (pcols(k), cols(k))
         return pltpu.make_async_remote_copy(
-            src_ref=concs[p].at[:, rows, pcols(k)], dst_ref=(clo if side == 0 else chi).at[p, :, rows, cols(k)],
+            src_ref=concs[p].at[:, rows, src], dst_ref=(clo if side == 0 else chi).at[p, :, rows, dst],
             send_sem=csend.at[p, side, k], recv_sem=crecv.at[p, side, k],
             device_id=after if side == 0 else before, device_id_type=MESH,
         )
@@ -214,7 +221,7 @@
         )
 
     def to_tile(a, k):
-        src, dst = (napl, napl_out) if a == 0 else (conc2, conc_out)
+        src, dst = (napl2, napl_out) if a == 0 else (conc2, conc_out)
         rows = pl.ds(pl.multiple_of(n * R, R), R)
         return pltpu.make_async_remote_copy(
             src_ref=src.at[:, :, cols(k)], dst_ref=dst.at[:, rows, :],
@@ -222,7 +229,7 @@
         )
 
     def from_tile(a, k):
-        src, dst = (napl, napl_out) if a == 0 else (conc2, conc_out)
+        src, dst = (napl2, napl_out) if a == 0 else (conc2, conc_out)
         rows = pl.ds(pl.multiple_of(k * R, R), R)
         return pltpu.make_async_remote_copy(
             src_ref=src.at[:, :, cols(k)], dst_ref=dst.at[:, rows, :],
@@ -230,7 +237,7 @@
         )
 
     def own_tile(a):
-        src, dst = (napl, napl_out) if a == 0 else (conc2, conc_out)
+        src, dst = (napl2, napl_out) if a == 0 else (conc2, conc_out)
         rows = pl.ds(pl.multiple_of(n * R, R), R)
         return pltpu.make_async_copy(src.at[:, :, cols(n)], dst.at[:, rows, :], own_sem.at[a])
 
@@ -243,8 +250,8 @@
         def _():
             own_tile(a).start()
 
-    def blocks(k, fn, carry=0):
-        return lax.fori_loop(0, per_chunk, lambda i, c: fn(k * per_chunk + i, c), carry)
+    def blocks(k, fn, carry=0, count=per_chunk):
+        return lax.fori_loop(0, count, lambda i, c: fn(k * count + i, c), carry)
 
     def at(b):
         return pl.ds(pl.multiple_of(b * B, B), B)
@@ -258,30 +265,29 @@
                 post0[SLOT[q], z, :, there] = out[q]
         return carry
 
+    per_part, ratio = part // B, parts // chunks
     smalls[0].wait()
     load(0).wait()
-    blocks(0, start_block)
+    blocks(0, start_block, 0, per_part)
     pl.semaphore_wait(barrier, narrow + 1)
     for side in range(2):
         edge(0, side, 0).start()
-    for copy in smalls[1:3]:
+
+    def first_part(k, carry):
+        @pl.when(lax.rem(k, ratio) == 0)
+        def _():
+            load(k // ratio).wait()
+
+        blocks(k, start_block, 0, per_part)
+        for side in range(2):
+            edge(0, side, k).start()
+        return carry
+
+    lax.fori_loop(1, parts, first_part, 0)
+    for copy in smalls[1:]:
         copy.wait()
     for side in range(2):
         poro_edge(side).start()
-
-    def first_chunk(k, carry):
-        load(k).wait()
-        blocks(k, start_block)
-        for side in range(2):
-            edge(0, side, k).start()
-        return carry
-
-    lax.fori_loop(1, chunks, first_chunk, 0)
-    for side in range(2):
-        for k in range(chunks):
-            conc_edge(0, side, k).start()
-    for copy in smalls[3:]:
-        copy.wait()
 
     def stream(post, s, z, b):
         base = b * B + B
@@ -319,7 +325,7 @@
             for side in range(2):
                 edge(s, side, k).wait_recv()
 
-        @pl.when(k < chunks - 1)
+        @pl.when(k < parts - 1)
         def _():
             for side in range(2):
                 edge(s, side, k + 1).wait_recv()
@@ -341,14 +347,17 @@
                 for side in range(2):
                     edge(s - 2, side, k).wait_send()
 
-            blocks(k, move_block)
+            blocks(k, move_block, 0, per_part)
             for side in range(2):
                 edge(s, side, k).start()
             return c
 
-        lax.fori_loop(0, chunks, chunk, 0)
+        lax.fori_loop(0, parts, chunk, 0)
 
         if s == 1:
+            for side in range(2):
+                conc_edge(0, side, 0).start()
+        if s == 2:
             for side in range(2):
                 poro_edge(side).wait_recv()
 
@@ -381,36 +390,28 @@
             uy[z, :, there] = jnp.where(solid, 0.0, jy * per)
             uz[z, :, here] = jnp.where(solid, 0.0, jz * per)
             for q in range(19):
-                fbuf[q, z, :, here] = jnp.where(solid, fbuf[q, z, :, here], f[q])
-        return carry
-
-    def store(k):
-        return pltpu.make_async_copy(
-            fbuf.at[:, :, :, cols(k)], pop_out.at[:, :, :, cols(k)], out_sem.at[k]
-        )
-
-    def last_chunk(k, carry):
+                pop_out[q, z, :, here] = jnp.where(solid, fbuf[q, z, :, here], f[q])
+        return carry
+
+    def last_part(k, carry):
         await_edges(STEPS - 1, k)
-        blocks(k, last_block)
-        for side in range(2):
-            vel_edge(side, k).start()
-        store(k).start()
-        return carry
-
-    lax.fori_loop(0, chunks, last_chunk, 0)
-
-    def transport(step, b, carry):
+        blocks(k, last_block, 0, per_part)
+
+        @pl.when(lax.rem(k, ratio) == ratio - 1)
+        def _():
+            for side in range(2):
+                vel_edge(side, k // ratio).start()
+
+        return carry
+
+    lax.fori_loop(0, parts, last_part, 0)
+
+    def inner_flux(step, b, carry):
         here, there, back, beyond = at(b), at(b + 1), at(b), at(b + 2)
         conc = concs[step]
         c = [conc[z, :, there] for z in range(Z)]
         if step == 0:
             for z in range(Z):
-                vx = ux[z, :, here]
-                high = jnp.where(last, pltpu.roll(vx, 1, 0), uhi[z, :, here])
-                low = jnp.where(first, pltpu.roll(vx, R - 1, 0), ulo[z, :, here])
-                nxt = pltpu.roll(vx, R - 1, 0)
-                ax[z, :, here] = wx[z, :, here] * (0.5 * (vx + jnp.where(row == R - 1, pltpu.roll(high, R - 1, 0), nxt)))
-                al[z, :, here] = wl[z, :, here] * (0.5 * (low + nxt))
                 vy = uy[z, :, there]
                 ay[z, :, here] = wy[z, :, here] * (
                     0.5 * (vy + pltpu.roll(jnp.where(lane == 0, uy[z, :, beyond], vy), B - 1, 1))
@@ -425,45 +426,62 @@
         flow = []
         for z in range(Z):
             own = c[z]
+            cb, cn = conc[z, :, back], conc[z, :, beyond]
+            left = pltpu.roll(jnp.where(lane == B - 1, cb, own), 1, 1)
+            right = pltpu.roll(jnp.where(lane == 0, cn, own), B - 1, 1)
+            right2 = pltpu.roll(jnp.where(lane < 2, cn, own), B - 2, 1)
+            yflux = face_flux(left, own, right, right2, wy[z, :, here], ay[z, :, here])
+            flow.append(yflux)
+            change = pltpu.roll(jnp.where(lane == B - 1, carry[z], yflux), 1, 1) - yflux
+            inner[z, :, here] = change + (zflux[(z - 1) % Z] - zflux[z])
+        return tuple(flow)
+
+    def transport(step, b, carry):
+        here, there = at(b), at(b + 1)
+        conc = concs[step]
+        for z in range(Z):
+            own = conc[z, :, there]
             high = chi[step, z, :, here]
-            low = clo[step, z, :, here]
+            low = jnp.where(first, 0.0, clo[step, z, :, here])
+            if step == 0:
+                vx = ux[z, :, here]
+                vhigh = jnp.where(last, pltpu.roll(vx, 1, 0), uhi[z, :, here])
+                vlow = jnp.where(first, pltpu.roll(vx, R - 1, 0), ulo[z, :, here])
+                nxt = pltpu.roll(vx, R - 1, 0)
+                a = wx[z, :, here] * (0.5 * (vx + jnp.where(row == R - 1, pltpu.roll(vhigh, R - 1, 0), nxt)))
+                e = wl[z, :, here] * (0.5 * (vlow + nxt))
+                ax[z, :, here] = a
+                al[z, :, here] = e
+            else:
+                a, e = ax[z, :, here], al[z, :, here]
             up1, up2 = pltpu.roll(own, R - 1, 0), pltpu.roll(own, R - 2, 0)
-            low = jnp.where(first, 0.0, low)
             down1 = pltpu.roll(jnp.where(row == R - 1, low, own), 1, 0)
             end = pltpu.roll(own, 1, 0)
             one = jnp.where(last, end, high)
             two = jnp.where(last, jnp.where(row == 0, end, pltpu.roll(own, 2, 0)), high)
             ahead = pltpu.roll(jnp.where(row == 0, one, own), R - 1, 0)
             far = pltpu.roll(jnp.where(row < 2, two, own), R - 2, 0)
-            xflux = face_flux(down1, own, ahead, far, wx[z, :, here], ax[z, :, here])
-            xlow = face_flux(pltpu.roll(low, 1, 0), low, up1, up2, wl[z, :, here], al[z, :, here])
+            xflux = face_flux(down1, own, ahead, far, wx[z, :, here], a)
+            xlow = face_flux(pltpu.roll(low, 1, 0), low, up1, up2, wl[z, :, here], e)
             change = pltpu.roll(jnp.where(row == R - 1, xlow, xflux), 1, 0) - xflux
-            cb, cn = conc[z, :, back], conc[z, :, beyond]
-            left = pltpu.roll(jnp.where(lane == B - 1, cb, own), 1, 1)
-            right = pltpu.roll(jnp.where(lane == 0, cn, own), B - 1, 1)
-            right2 = pltpu.roll(jnp.where(lane < 2, cn, own), B - 2, 1)
-            yflux = face_flux(left, own, right, right2, wy[z, :, here], ay[z, :, here])
-            flow.append(yflux)
-            change = change + (pltpu.roll(jnp.where(lane == B - 1, carry[z], yflux), 1, 1) - yflux)
-            change = change + (zflux[(z - 1) % Z] - zflux[z])
-            s = napl[z, :, here]
+            change = change + inner[z, :, here]
             if step == 0:
+                s = napl[z, :, here]
                 rate = 0.3 * s * (1.0 - own)
                 new = own + (change + rate) * inv[z, :, here]
                 conc1[z, :, there] = new
                 s = s - 0.5 * rate
                 rate = 0.3 * s * (1.0 - new)
-                napl[z, :, here] = s - 0.5 * rate
+                napl2[z, :, here] = s - 0.5 * rate
                 rate_buf[z, :, here] = rate
             else:
                 conc2[z, :, here] = own + (change + rate_buf[z, :, here]) * inv[z, :, here]
-        return tuple(flow)
+        return carry
 
     def first_transport(k, carry):
         for side in range(2):
             vel_edge(side, k).wait_recv()
-            conc_edge(0, side, k).wait_recv()
-        carry = blocks(k, functools.partial(transport, 0), carry)
+        blocks(k, functools.partial(transport, 0))
         for side in range(2):
             conc_edge(1, side, k).start()
         send_tile(0, k)
@@ -472,27 +490,35 @@
     def second_transport(k, carry):
         for side in range(2):
             conc_edge(1, side, k).wait_recv()
-        carry = blocks(k, functools.partial(transport, 1), carry)
+        blocks(k, functools.partial(transport, 1))
         send_tile(1, k)
         return carry
 
     still = (zero,) * Z
-    lax.fori_loop(0, chunks, first_transport, still)
-    lax.fori_loop(0, chunks, second_transport, still)
-
-    def settle(k, carry):
+    lax.fori_loop(0, width // B, functools.partial(inner_flux, 0), still)
+    for side in range(2):
+        conc_edge(0, side, 0).wait_recv()
+    lax.fori_loop(0, chunks, first_transport, 0)
+    lax.fori_loop(0, width // B, functools.partial(inner_flux, 1), still)
+    lax.fori_loop(0, chunks, second_transport, 0)
+
+    def settle_part(k, carry):
         for side in range(2):
             for s in (STEPS - 2, STEPS - 1):
                 edge(s, side, k).wait_send()
+        return carry
+
+    def settle(k, carry):
+        for side in range(2):
             vel_edge(side, k).wait_send()
-            for p in range(2):
-                conc_edge(p, side, k).wait_send()
-        store(k).wait()
-        return carry
-
+            conc_edge(1, side, k).wait_send()
+        return carry
+
+    lax.fori_loop(0, parts, settle_part, 0)
     lax.fori_loop(0, chunks, settle, 0)
     for side in range(2):
         poro_edge(side).wait_send()
+        conc_edge(0, side, 0).wait_send()
 
     def settle_tile(k, carry):
         @pl.when(k != n)
@@ -525,7 +551,7 @@
         pltpu.VMEM((Z, R, padded), f32),
         full(),
         pltpu.VMEM((Z, R, padded), f32), pltpu.VMEM((Z, R, padded), f32),
-        full(), full(),
+        full(), full(), full(), full(),
         pltpu.VMEM((2, Z, width), jnp.int32),
         pltpu.VMEM((19, Z, R, padded), f32), pltpu.VMEM((19, Z, R, padded), f32),
         pltpu.VMEM((STEPS, 5, Z, R, padded), f32),
@@ -537,8 +563,8 @@
         full(), full(), full(), full(),
         full(), full(), full(), full(),
         full(),
-        DMA((narrow,)), DMA((5,)), DMA((narrow,)), DMA((2,)),
-        DMA((STEPS, 2, narrow)), DMA((STEPS, 2, narrow)),
+        DMA((narrow,)), DMA((5,)), DMA((2,)),
+        DMA((STEPS, 2, PARTS)), DMA((STEPS, 2, PARTS)),
         DMA((2,)), DMA((2,)),
         DMA((2, 2, narrow)), DMA((2, 2, narrow)),
         DMA((2, narrow)), DMA((2, narrow)),
@@ -547,9 +573,9 @@
     tiles = jax.ShapeDtypeStruct((Z, R * narrow, tile), f32)
     return pl.pallas_call(
         functools.partial(body, wide, narrow, width, tile),
-        out_shape=(jax.ShapeDtypeStruct(populations.shape, f32), tiles, tiles),
+        out_shape=(pltpu.VMEM(populations.shape, f32),) + (pltpu.VMEM(tiles.shape, f32),) * 2,
         in_specs=[any_space] * 6,
-        out_specs=(any_space,) * 3,
+        out_specs=(pl.BlockSpec(memory_space=pltpu.VMEM),) * 3,
         scratch_shapes=scratch,
         compiler_params=pltpu.CompilerParams(
             collective_id=0, has_side_effects=True, vmem_limit_bytes=56 * 2**20

time: 57.1 us -> 52.7 us (0.923)
  local copies, waits for them, and re-layouts: 6.76 us -> 3.68 us
  Pallas kernels: 49.6 us -> 48.3 us
    unnamed x7 -> x3, local copies, waits for them, and re-layouts: 6.76 us -> 3.68 us
    pallas_call x1, Pallas kernels: 49.6 us -> 48.3 us  [local(): pl.pallas_call(functools.partial(body, wide, narrow, width, tile), out_sh...]
where the time goes in v2:
time: 52.7 us; the launch traced here: 52.6 us
  Pallas kernels  48.3 us (92%)
  local copies, waits for them, and re-layouts  3.68 us (7%)
  between operations  0.64 us (1%)
    pallas_call x1, Pallas kernels, local(): pl.pallas_call(functools.partial(body, wide, narrow, width, tile), out_sh...  48.3 us
    unnamed x3, local copies, waits for them, and re-layouts  3.68 us

profile of v2, /device:TPU:56, one launch (start us, length us, event | category | flops | bytes accessed | tf_op | source)
XLA Modules:
  0.0 52.6 jit_solution(1693603787635567722)
XLA Ops:
  0.6 48.3 %dissolution.1 = (f32[19,4,8,2048]{3,2,1,0:T(8,128)S(1)}, f32[4,64,256]{2,1,0:T(8,128)S(1)}, f32[4,64,256]{2,1,0:T(8,128)S(1)}) custom-call(f32[19,4,8,2048]{3,2,1,0:T(8,128)} %pop_in.1, s32[4,8,2048]{2,1,0:T(8,128)} %phase_in.1, f32[4,8,2048]{2,1,0:T(8,128)} %poro_in.1, f32[4,8,2048]{2,1,0:T(8,128)} %napl_in.1, f32[4,8,2048]{2,1,0:T(8,128)} %conc_in.1, ...), custom_call_target="tpu_custom_call" | custom-call | tf_op jit(solution)/shard_map/dissolution/pallas_call | solution.py:574
  48.9 2.3 %copy.12 = f32[19,4,8,2048]{3,2,1,0:T(8,128)} copy(f32[19,4,8,2048]{3,2,1,0:T(8,128)S(1)} %get-tuple-element.3) | data formatting | bytes 9961472
  51.2 0.7 %copy.13 = f32[4,64,256]{2,1,0:T(8,128)} copy(f32[4,64,256]{2,1,0:T(8,128)S(1)} %get-tuple-element.4) | data formatting | bytes 524288
  51.9 0.7 %copy.14 = f32[4,64,256]{2,1,0:T(8,128)} copy(f32[4,64,256]{2,1,0:T(8,128)S(1)} %get-tuple-element.5) | data formatting | bytes 524288

commit v3 on v2

--- a/solution.py
+++ b/solution.py
@@ -121,6 +121,14 @@
     after, before = neighbour(1), neighbour(-1)
     first, last = strip == 0, strip == wide * narrow - 1
 
+    barrier = pltpu.get_barrier_semaphore()
+    pl.semaphore_signal(barrier, inc=1, device_id=after, device_id_type=MESH)
+    pl.semaphore_signal(barrier, inc=1, device_id=before, device_id_type=MESH)
+    for k in range(1, narrow):
+        pl.semaphore_signal(
+            barrier, inc=1, device_id=(w, lax.rem(n + k, narrow)), device_id_type=MESH
+        )
+
     def part_cols(k):
         return pl.ds(pl.multiple_of(B + k * part, B), part)
 
@@ -148,14 +156,6 @@
         copy.start()
     for k in range(1, chunks):
         load(k).start()
-
-    barrier = pltpu.get_barrier_semaphore()
-    pl.semaphore_signal(barrier, inc=1, device_id=after, device_id_type=MESH)
-    pl.semaphore_signal(barrier, inc=1, device_id=before, device_id_type=MESH)
-    for k in range(1, narrow):
-        pl.semaphore_signal(
-            barrier, inc=1, device_id=(w, lax.rem(n + k, narrow)), device_id_type=MESH
-        )
 
     lane = lax.broadcasted_iota(jnp.int32, (R, B), 1)
     row = lax.broadcasted_iota(jnp.int32, (R, B), 0)
@@ -220,6 +220,15 @@
             device_id=after if side == 0 else before, device_id_type=MESH,
         )
 
+    def start_open(side, copy):
+        pl.when(jnp.logical_not(last if side == 0 else first))(copy.start)
+
+    def sent_open(side, copy):
+        pl.when(jnp.logical_not(last if side == 0 else first))(copy.wait_send)
+
+    def await_open(side, copy):
+        pl.when(jnp.logical_not(first if side == 0 else last))(copy.wait_recv)
+
     def to_tile(a, k):
         src, dst = (napl2, napl_out) if a == 0 else (conc2, conc_out)
         rows = pl.ds(pl.multiple_of(n * R, R), R)
@@ -251,7 +260,7 @@
             own_tile(a).start()
 
     def blocks(k, fn, carry=0, count=per_chunk):
-        return lax.fori_loop(0, count, lambda i, c: fn(k * count + i, c), carry)
+        return lax.fori_loop(0, count, lambda i, c: fn(k * count + i, c), carry, unroll=True)
 
     def at(b):
         return pl.ds(pl.multiple_of(b * B, B), B)
@@ -286,8 +295,40 @@
     lax.fori_loop(1, parts, first_part, 0)
     for copy in smalls[1:]:
         copy.wait()
+    def each_block(fn):
+        def one(b, carry):
+            for z in range(Z):
+                fn(z, at(b), at(b + 1))
+            return carry
+
+        lax.fori_loop(0, width // B, one, 0)
+
+    def inlet(z, here, there):
+        plo[z, :, here] = jnp.broadcast_to(flags[0, z : z + 1, here].astype(jnp.float32), (R, B))
+        for p in range(2):
+            clo[p, z, :, here] = zero
+
+    def outlet(z, here, there):
+        phi[z, :, here] = jnp.broadcast_to(flags[1, z : z + 1, here].astype(jnp.float32), (R, B))
+
+    def outlet_conc(p):
+        def fill_rows(z, here, there):
+            own = concs[p][z, :, there]
+            chi[p, z, :, here] = jnp.where(row == 0, pltpu.roll(own, 1, 0), pltpu.roll(own, 2, 0))
+
+        pl.when(last)(lambda: each_block(fill_rows))
+
+    def inlet_vel(z, here, there):
+        ulo[z, :, here] = pltpu.roll(ux[z, :, here], R - 1, 0)
+
+    def outlet_vel(z, here, there):
+        uhi[z, :, here] = pltpu.roll(ux[z, :, here], 1, 0)
+
+    pl.when(first)(lambda: each_block(inlet))
+    pl.when(last)(lambda: each_block(outlet))
+    outlet_conc(0)
     for side in range(2):
-        poro_edge(side).start()
+        start_open(side, poro_edge(side))
 
     def stream(post, s, z, b):
         base = b * B + B
@@ -356,17 +397,16 @@
 
         if s == 1:
             for side in range(2):
-                conc_edge(0, side, 0).start()
+                start_open(side, conc_edge(0, side, 0))
         if s == 2:
             for side in range(2):
-                poro_edge(side).wait_recv()
+                await_open(side, poro_edge(side))
 
             def coef(b, c):
                 here, there, beyond = at(b), at(b + 1), at(b + 2)
                 for z in range(Z):
                     own = poro[z, :, there]
-                    high = jnp.where(last, flags[1, z : z + 1, here].astype(jnp.float32), phi[z, :, here])
-                    low = jnp.where(first, flags[0, z : z + 1, here].astype(jnp.float32), plo[z, :, here])
+                    high, low = phi[z, :, here], plo[z, :, here]
                     wx[z, :, here] = own * pltpu.roll(jnp.where(row == 0, high, own), R - 1, 0)
                     wl[z, :, here] = low * pltpu.roll(own, R - 1, 0)
                     wy[z, :, here] = own * pltpu.roll(jnp.where(lane == 0, poro[z, :, beyond], own), B - 1, 1)
@@ -374,7 +414,7 @@
                     inv[z, :, here] = 1.0 / jnp.maximum(own, 0.3)
                 return c
 
-            lax.fori_loop(0, width // B, coef, 0)
+            lax.fori_loop(0, width // B, coef, 0, unroll=2)
 
     for s in range(1, STEPS):
         one_step(s)
@@ -400,7 +440,7 @@
         @pl.when(lax.rem(k, ratio) == ratio - 1)
         def _():
             for side in range(2):
-                vel_edge(side, k // ratio).start()
+                start_open(side, vel_edge(side, k // ratio))
 
         return carry
 
@@ -442,25 +482,20 @@
         for z in range(Z):
             own = conc[z, :, there]
             high = chi[step, z, :, here]
-            low = jnp.where(first, 0.0, clo[step, z, :, here])
+            low = clo[step, z, :, here]
             if step == 0:
                 vx = ux[z, :, here]
-                vhigh = jnp.where(last, pltpu.roll(vx, 1, 0), uhi[z, :, here])
-                vlow = jnp.where(first, pltpu.roll(vx, R - 1, 0), ulo[z, :, here])
-                nxt = pltpu.roll(vx, R - 1, 0)
-                a = wx[z, :, here] * (0.5 * (vx + jnp.where(row == R - 1, pltpu.roll(vhigh, R - 1, 0), nxt)))
-                e = wl[z, :, here] * (0.5 * (vlow + nxt))
+                nxt = pltpu.roll(jnp.where(row == 0, uhi[z, :, here], vx), R - 1, 0)
+                a = wx[z, :, here] * (0.5 * (vx + nxt))
+                e = wl[z, :, here] * (0.5 * (ulo[z, :, here] + pltpu.roll(vx, R - 1, 0)))
                 ax[z, :, here] = a
                 al[z, :, here] = e
             else:
                 a, e = ax[z, :, here], al[z, :, here]
             up1, up2 = pltpu.roll(own, R - 1, 0), pltpu.roll(own, R - 2, 0)
             down1 = pltpu.roll(jnp.where(row == R - 1, low, own), 1, 0)
-            end = pltpu.roll(own, 1, 0)
-            one = jnp.where(last, end, high)
-            two = jnp.where(last, jnp.where(row == 0, end, pltpu.roll(own, 2, 0)), high)
-            ahead = pltpu.roll(jnp.where(row == 0, one, own), R - 1, 0)
-            far = pltpu.roll(jnp.where(row < 2, two, own), R - 2, 0)
+            ahead = pltpu.roll(jnp.where(row == 0, high, own), R - 1, 0)
+            far = pltpu.roll(jnp.where(row < 2, high, own), R - 2, 0)
             xflux = face_flux(down1, own, ahead, far, wx[z, :, here], a)
             xlow = face_flux(pltpu.roll(low, 1, 0), low, up1, up2, wl[z, :, here], e)
             change = pltpu.roll(jnp.where(row == R - 1, xlow, xflux), 1, 0) - xflux
@@ -480,26 +515,29 @@
 
     def first_transport(k, carry):
         for side in range(2):
-            vel_edge(side, k).wait_recv()
+            await_open(side, vel_edge(side, k))
         blocks(k, functools.partial(transport, 0))
         for side in range(2):
-            conc_edge(1, side, k).start()
+            start_open(side, conc_edge(1, side, k))
         send_tile(0, k)
         return carry
 
     def second_transport(k, carry):
         for side in range(2):
-            conc_edge(1, side, k).wait_recv()
+            await_open(side, conc_edge(1, side, k))
         blocks(k, functools.partial(transport, 1))
         send_tile(1, k)
         return carry
 
     still = (zero,) * Z
-    lax.fori_loop(0, width // B, functools.partial(inner_flux, 0), still)
+    lax.fori_loop(0, width // B, functools.partial(inner_flux, 0), still, unroll=4)
     for side in range(2):
-        conc_edge(0, side, 0).wait_recv()
+        await_open(side, conc_edge(0, side, 0))
+    pl.when(first)(lambda: each_block(inlet_vel))
+    pl.when(last)(lambda: each_block(outlet_vel))
     lax.fori_loop(0, chunks, first_transport, 0)
-    lax.fori_loop(0, width // B, functools.partial(inner_flux, 1), still)
+    outlet_conc(1)
+    lax.fori_loop(0, width // B, functools.partial(inner_flux, 1), still, unroll=4)
     lax.fori_loop(0, chunks, second_transport, 0)
 
     def settle_part(k, carry):
@@ -510,15 +548,15 @@
 
     def settle(k, carry):
         for side in range(2):
-            vel_edge(side, k).wait_send()
-            conc_edge(1, side, k).wait_send()
+            sent_open(side, vel_edge(side, k))
+            sent_open(side, conc_edge(1, side, k))
         return carry
 
     lax.fori_loop(0, parts, settle_part, 0)
     lax.fori_loop(0, chunks, settle, 0)
     for side in range(2):
-        poro_edge(side).wait_send()
-        conc_edge(0, side, 0).wait_send()
+        sent_open(side, poro_edge(side))
+        sent_open(side, conc_edge(0, side, 0))
 
     def settle_tile(k, carry):
         @pl.when(k != n)

time: 52.7 us -> 48.8 us (0.926)
  Pallas kernels: 48.3 us -> 44.1 us
    pallas_call x1, Pallas kernels: 48.3 us -> 44.1 us  [local(): pl.pallas_call(functools.partial(body, wide, narrow, width, tile), out_sh...]
where the time goes in v3:
time: 48.8 us; the launch traced here: 48.4 us
  Pallas kernels  44.1 us (90%)
  local copies, waits for them, and re-layouts  3.68 us (8%)
  between operations  0.64 us (1%)
    pallas_call x1, Pallas kernels, local(): pl.pallas_call(functools.partial(body, wide, narrow, width, tile), out_sh...  44.1 us
    unnamed x3, local copies, waits for them, and re-layouts  3.68 us

profile of v3, /device:TPU:56, one launch (start us, length us, event | category | flops | bytes accessed | tf_op | source)
XLA Modules:
  0.0 48.4 jit_solution(4462568961586929945)
XLA Ops:
  0.6 44.1 %dissolution.1 = (f32[19,4,8,2048]{3,2,1,0:T(8,128)S(1)}, f32[4,64,256]{2,1,0:T(8,128)S(1)}, f32[4,64,256]{2,1,0:T(8,128)S(1)}) custom-call(f32[19,4,8,2048]{3,2,1,0:T(8,128)} %pop_in.1, s32[4,8,2048]{2,1,0:T(8,128)} %phase_in.1, f32[4,8,2048]{2,1,0:T(8,128)} %poro_in.1, f32[4,8,2048]{2,1,0:T(8,128)} %napl_in.1, f32[4,8,2048]{2,1,0:T(8,128)} %conc_in.1, ...), custom_call_target="tpu_custom_call" | custom-call | tf_op jit(solution)/shard_map/dissolution/pallas_call | solution.py:612
  44.7 2.3 %copy.12 = f32[19,4,8,2048]{3,2,1,0:T(8,128)} copy(f32[19,4,8,2048]{3,2,1,0:T(8,128)S(1)} %get-tuple-element.3) | data formatting | bytes 9961472
  47.0 0.7 %copy.13 = f32[4,64,256]{2,1,0:T(8,128)} copy(f32[4,64,256]{2,1,0:T(8,128)S(1)} %get-tuple-element.4) | data formatting | bytes 524288
  47.7 0.7 %copy.14 = f32[4,64,256]{2,1,0:T(8,128)} copy(f32[4,64,256]{2,1,0:T(8,128)S(1)} %get-tuple-element.5) | data formatting | bytes 524288

commit v4 on v3

--- a/solution.py
+++ b/solution.py
@@ -19,7 +19,7 @@
 ORDER = UP + DOWN + [0, 3, 4, 5, 6, 15, 16, 17, 18]
 SLOT = {q: i for i, q in enumerate(ORDER)}
 STEPS = 4
-PARTS = 8
+PARTS = 16
 Z = 4
 R = 8
 B = 128
@@ -152,10 +152,10 @@
     ]
     smalls[0].start()
     load(0).start()
+    for k in range(1, chunks):
+        load(k).start()
     for copy in smalls[1:]:
         copy.start()
-    for k in range(1, chunks):
-        load(k).start()
 
     lane = lax.broadcasted_iota(jnp.int32, (R, B), 1)
     row = lax.broadcasted_iota(jnp.int32, (R, B), 0)
@@ -179,8 +179,6 @@
                 concs[p][z, :, end] = zero
         return carry
 
-    lax.fori_loop(0, Z, fill, 0)
-
     def edge(s, side, k):
         post = posts[s % 2]
         if side == 0:
@@ -293,6 +291,7 @@
         return carry
 
     lax.fori_loop(1, parts, first_part, 0)
+    lax.fori_loop(0, Z, fill, 0)
     for copy in smalls[1:]:
         copy.wait()
     def each_block(fn):
@@ -519,7 +518,6 @@
         blocks(k, functools.partial(transport, 0))
         for side in range(2):
             start_open(side, conc_edge(1, side, k))
-        send_tile(0, k)
         return carry
 
     def second_transport(k, carry):
@@ -527,6 +525,10 @@
             await_open(side, conc_edge(1, side, k))
         blocks(k, functools.partial(transport, 1))
         send_tile(1, k)
+        return carry
+
+    def send_napl(k, carry):
+        send_tile(0, lax.rem(n + k, chunks))
         return carry
 
     still = (zero,) * Z
@@ -536,6 +538,7 @@
     pl.when(first)(lambda: each_block(inlet_vel))
     pl.when(last)(lambda: each_block(outlet_vel))
     lax.fori_loop(0, chunks, first_transport, 0)
+    lax.fori_loop(0, chunks, send_napl, 0)
     outlet_conc(1)
     lax.fori_loop(0, width // B, functools.partial(inner_flux, 1), still, unroll=4)
     lax.fori_loop(0, chunks, second_transport, 0)

time: 48.8 us -> 48.4 us (level)
  Pallas kernels: 44.1 us -> 43.5 us
    pallas_call x1, Pallas kernels: 44.1 us -> 43.5 us  [local(): pl.pallas_call(functools.partial(body, wide, narrow, width, tile), out_sh...]
where the time goes in v4:
time: 48.4 us; the launch traced here: 47.9 us
  Pallas kernels  43.5 us (90%)
  local copies, waits for them, and re-layouts  3.68 us (8%)
  between operations  0.64 us (1%)
    pallas_call x1, Pallas kernels, local(): pl.pallas_call(functools.partial(body, wide, narrow, width, tile), out_sh...  43.5 us
    unnamed x3, local copies, waits for them, and re-layouts  3.68 us

profile of v4, /device:TPU:56, one launch (start us, length us, event | category | flops | bytes accessed | tf_op | source)
XLA Modules:
  0.0 47.9 jit_solution(7632232108493954642)
XLA Ops:
  0.6 43.5 %dissolution.1 = (f32[19,4,8,2048]{3,2,1,0:T(8,128)S(1)}, f32[4,64,256]{2,1,0:T(8,128)S(1)}, f32[4,64,256]{2,1,0:T(8,128)S(1)}) custom-call(f32[19,4,8,2048]{3,2,1,0:T(8,128)} %pop_in.1, s32[4,8,2048]{2,1,0:T(8,128)} %phase_in.1, f32[4,8,2048]{2,1,0:T(8,128)} %poro_in.1, f32[4,8,2048]{2,1,0:T(8,128)} %napl_in.1, f32[4,8,2048]{2,1,0:T(8,128)} %conc_in.1, ...), custom_call_target="tpu_custom_call" | custom-call | tf_op jit(solution)/shard_map/dissolution/pallas_call | solution.py:615
  44.2 2.3 %copy.12 = f32[19,4,8,2048]{3,2,1,0:T(8,128)} copy(f32[19,4,8,2048]{3,2,1,0:T(8,128)S(1)} %get-tuple-element.3) | data formatting | bytes 9961472
  46.4 0.7 %copy.13 = f32[4,64,256]{2,1,0:T(8,128)} copy(f32[4,64,256]{2,1,0:T(8,128)S(1)} %get-tuple-element.4) | data formatting | bytes 524288
  47.1 0.7 %copy.14 = f32[4,64,256]{2,1,0:T(8,128)} copy(f32[4,64,256]{2,1,0:T(8,128)S(1)} %get-tuple-element.5) | data formatting | bytes 524288

commit v5 on v4

--- a/solution.py
+++ b/solution.py
@@ -537,11 +537,11 @@
         await_open(side, conc_edge(0, side, 0))
     pl.when(first)(lambda: each_block(inlet_vel))
     pl.when(last)(lambda: each_block(outlet_vel))
-    lax.fori_loop(0, chunks, first_transport, 0)
+    lax.fori_loop(0, chunks, first_transport, 0, unroll=2)
     lax.fori_loop(0, chunks, send_napl, 0)
     outlet_conc(1)
     lax.fori_loop(0, width // B, functools.partial(inner_flux, 1), still, unroll=4)
-    lax.fori_loop(0, chunks, second_transport, 0)
+    lax.fori_loop(0, chunks, second_transport, 0, unroll=2)
 
     def settle_part(k, carry):
         for side in range(2):

time: 48.4 us -> 48.4 us (level)
  no operation moved by 1% of the time
where the time goes in v5:
time: 48.4 us; the launch traced here: 47.9 us
  Pallas kernels  43.5 us (90%)
  local copies, waits for them, and re-layouts  3.68 us (8%)
  between operations  0.64 us (1%)
    pallas_call x1, Pallas kernels, local(): pl.pallas_call(functools.partial(body, wide, narrow, width, tile), out_sh...  43.5 us
    unnamed x3, local copies, waits for them, and re-layouts  3.68 us

profile of v5, /device:TPU:56, one launch (start us, length us, event | category | flops | bytes accessed | tf_op | source)
XLA Modules:
  0.0 47.9 jit_solution(17404962058597301496)
XLA Ops:
  0.6 43.5 %dissolution.1 = (f32[19,4,8,2048]{3,2,1,0:T(8,128)S(1)}, f32[4,64,256]{2,1,0:T(8,128)S(1)}, f32[4,64,256]{2,1,0:T(8,128)S(1)}) custom-call(f32[19,4,8,2048]{3,2,1,0:T(8,128)} %pop_in.1, s32[4,8,2048]{2,1,0:T(8,128)} %phase_in.1, f32[4,8,2048]{2,1,0:T(8,128)} %poro_in.1, f32[4,8,2048]{2,1,0:T(8,128)} %napl_in.1, f32[4,8,2048]{2,1,0:T(8,128)} %conc_in.1, ...), custom_call_target="tpu_custom_call" | custom-call | tf_op jit(solution)/shard_map/dissolution/pallas_call | solution.py:615
  44.2 2.3 %copy.12 = f32[19,4,8,2048]{3,2,1,0:T(8,128)} copy(f32[19,4,8,2048]{3,2,1,0:T(8,128)S(1)} %get-tuple-element.3) | data formatting | bytes 9961472
  46.4 0.7 %copy.13 = f32[4,64,256]{2,1,0:T(8,128)} copy(f32[4,64,256]{2,1,0:T(8,128)S(1)} %get-tuple-element.4) | data formatting | bytes 524288
  47.2 0.7 %copy.14 = f32[4,64,256]{2,1,0:T(8,128)} copy(f32[4,64,256]{2,1,0:T(8,128)S(1)} %get-tuple-element.5) | data formatting | bytes 524288
